TPU v7x, 32 devices: a whole 2x2x4 slice. The times are simulated.
32 devices in a mesh: group: 16 (over z, y, core), tp: 2 (over x).
Axes of the slice: x: 2, y: 2, z: 4, core: 2. Of those that a mesh axis runs over, the one named last changes fastest.
Arguments:
- queries: bfloat16 [1024, 2048], P('group', 'tp'), may hold values from -22 to 22
- new_kv: bfloat16 [1024, 1024], P('group', 'tp'), may hold values from -6 to 6
- local_cache: bfloat16 [4096, 1024], P('group', 'tp'), may hold values from -6 to 6
- remote_pool: bfloat16 [2048, 1024], P('group', 'tp'), may hold values from -6 to 6
- page_index: int32 [16, 16], P('group'), may hold values from 0 to 15, each once within a row
- lengths: int32 [16], P('group'), may hold values from 256 to 384, as said below
- sinks: float32 [32], P('tp'), may hold values from 4 to 8
- out_weight: bfloat16 [2048, 2880], P('tp'), may hold values from -0.125 to 0.125
- residual: bfloat16 [1024, 2880], P('group', 'tp'), may hold values from -6 to 6
- norm_gain: float32 [2880], replicated, may hold values from 0.5 to 2
- routes: int32 [1024, 4], P('group'), may hold values from 0 to 7, all different within a row; in each aligned block of 64 rows (0 to 63, 64 to 127, ...) at most 40 rows name the same one
- route_weights: float32 [1024, 4], P('group'), may hold values from 0.1 to 1
- expert_gate: bfloat16 [16, 2880, 1440], P('group', None, 'tp'), may hold values from -0.109375 to 0.109375
- expert_up: bfloat16 [16, 2880, 1440], P('group', None, 'tp'), may hold values from -0.109375 to 0.109375
- expert_down: bfloat16 [16, 1440, 2880], P('group', None, 'tp'), may hold values from -0.109375 to 0.109375
Outputs:
- layer_out: bfloat16 [1024, 2880], P('group', 'tp')
Inputs may be any that keep to these rules, and one draw needn't show every extreme that they name: `lengths`: every request has at least 256 cached positions; some request has exactly 256, some exactly 384. `routes`: within the rows of one request no expert is named by more than 40 rows. `page_index`: each row is a permutation.
All inputs are finite; a program needn't handle non-finite values.
Results may differ from a plain program's by a relative error of at most 0.013.
Values may be sent and summed in bfloat16 or wider, within the bound.
No kernel may reach another device: no remote copies, remote signals or barrier semaphores. Data moves between devices by JAX's collectives and lax.ppermute only.
A program may use at most 128 MiB of HBM per device.

v0:
```python
import jax
import jax.numpy as jnp
from jax import lax
from jax.sharding import PartitionSpec as P

HEAD = 64


THETA = 150000.0
ALPHA = 1.702
EPSILON = 1e-05


def rotate(values, positions):
    half_dim = values.shape[-1] // 2
    inverse = THETA ** (-2.0 * jnp.arange(half_dim, dtype=jnp.float32) / values.shape[-1])
    angles = positions[:, None, None] * inverse[None, None, :]
    cosine = jnp.cos(angles)
    sine_part = jnp.sin(angles)
    first_part = values[..., :half_dim]
    second_part = values[..., half_dim:]
    return jnp.concatenate(
        [
            first_part * cosine - second_part * sine_part,
            second_part * cosine + first_part * sine_part,
        ],
        axis=-1,
    )


def attend(query_rows, kv_rows, cache_kv, cache_valid, sinks, length):
    block_len = query_rows.shape[0]
    kv_heads = kv_rows.shape[1] // (2 * HEAD)
    query_heads = query_rows.shape[1] // HEAD
    group_size = query_heads // kv_heads
    positions = (length + jnp.arange(block_len, dtype=jnp.int32)).astype(jnp.float32)
    query_rot = rotate(
        query_rows.astype(jnp.float32).reshape(block_len, query_heads, HEAD), positions
    ).astype(jnp.bfloat16)
    kv_parts = kv_rows.reshape(block_len, kv_heads, 2, HEAD)
    key_rot = rotate(kv_parts[:, :, 0].astype(jnp.float32), positions).astype(jnp.bfloat16)
    cache_parts = cache_kv.reshape(cache_kv.shape[0], kv_heads, 2, HEAD)
    all_keys = jnp.concatenate([cache_parts[:, :, 0], key_rot], axis=0)
    all_values = jnp.concatenate([cache_parts[:, :, 1], kv_parts[:, :, 1]], axis=0)
    token_order = jnp.arange(block_len, dtype=jnp.int32)
    causal = token_order[None, :] <= token_order[:, None]
    allowed = jnp.concatenate(
        [jnp.broadcast_to(cache_valid[None, :], (block_len, cache_valid.shape[0])), causal], axis=1
    )
    row_allowed = jnp.repeat(allowed, group_size, axis=0)
    score_scale = HEAD ** (-0.5)
    outputs = []
    for kv_head in range(kv_heads):
        query_block = query_rot[:, kv_head * group_size : (kv_head + 1) * group_size].reshape(
            block_len * group_size, HEAD
        )
        scores = (
            jnp.dot(query_block, all_keys[:, kv_head].T, preferred_element_type=jnp.float32)
            * score_scale
        )
        scores = jnp.where(row_allowed, scores, -jnp.inf)
        sink_rows = jnp.tile(sinks[kv_head * group_size : (kv_head + 1) * group_size], block_len)
        row_max = jnp.maximum(jnp.max(scores, axis=1), sink_rows)
        weights = jnp.exp(scores - row_max[:, None])
        denominator = jnp.sum(weights, axis=1) + jnp.exp(sink_rows - row_max)
        blended = (
            jnp.dot(
                weights.astype(jnp.bfloat16),
                all_values[:, kv_head],
                preferred_element_type=jnp.float32,
            )
            / denominator[:, None]
        )
        outputs.append(blended.astype(jnp.bfloat16).reshape(block_len, group_size * HEAD))
    return jnp.concatenate(outputs, axis=1)


def on_device(
    queries,
    new_kv,
    local_cache,
    remote_pool,
    page_index,
    lengths,
    sinks,
    out_weight,
    residual,
    norm_gain,
    routes,
    route_weights,
    expert_gate,
    expert_up,
    expert_down,
):
    groups = lax.axis_size("group")
    lane_count = remote_pool.shape[1]
    local_len = local_cache.shape[0]
    fetched = lax.all_to_all(
        remote_pool.reshape(groups, -1, lane_count),
        "group",
        split_axis=0,
        concat_axis=0,
        tiled=True,
    )
    page_len = fetched.shape[1]
    length = lengths[0]
    offsets = jnp.arange(page_len, dtype=jnp.int32)
    remote_pos = local_len + page_index[0][:, None] * page_len + offsets[None, :]
    cache_valid = jnp.concatenate(
        [jnp.ones((local_len,), jnp.bool_), (remote_pos < length).reshape(-1)]
    )
    cache_kv = jnp.concatenate([local_cache, fetched.reshape(-1, lane_count)], axis=0)
    attended = attend(queries, new_kv, cache_kv, cache_valid, sinks, length)
    width = residual.shape[1]
    start = lax.axis_index("tp") * width
    own_gain = lax.dynamic_slice_in_dim(norm_gain, start, width, 0)
    partial_sum = jnp.dot(attended, out_weight, preferred_element_type=jnp.float32)
    own_cols = lax.dynamic_slice_in_dim(partial_sum, start, width, 1) + residual.astype(jnp.float32)
    partial_sum = lax.dynamic_update_slice_in_dim(partial_sum, own_cols, start, 1)
    hidden_state = lax.psum(partial_sum, "tp")
    mean_square = jnp.mean(hidden_state * hidden_state, axis=1, keepdims=True)
    own_state = lax.dynamic_slice_in_dim(hidden_state, start, width, 1)
    normed_own = (own_state * lax.rsqrt(mean_square + EPSILON) * own_gain).astype(jnp.bfloat16)
    block_len = normed_own.shape[0]
    top_count = routes.shape[1]
    experts = groups // 2
    capacity = 5 * block_len * top_count // (4 * experts)
    member = jnp.any(
        routes[:, :, None] == jnp.arange(experts, dtype=jnp.int32)[None, None, :], axis=1
    ).astype(jnp.int32)
    slot_rank = jnp.cumsum(member, axis=0) - member
    slot_hit = member[:, :, None] * (
        slot_rank[:, :, None] == jnp.arange(capacity, dtype=jnp.int32)[None, None, :]
    ).astype(jnp.int32)
    slot_token = jnp.sum(slot_hit * jnp.arange(block_len, dtype=jnp.int32)[:, None, None], axis=0)
    slot_valid = jnp.sum(slot_hit, axis=0)
    send_own = jnp.take(normed_own, slot_token.reshape(-1), axis=0) * slot_valid.reshape(
        -1, 1
    ).astype(jnp.bfloat16)
    hidden_part = expert_gate.shape[2]
    gate_and_up = jnp.concatenate([expert_gate[0], expert_up[0]], axis=1)
    outgoing = send_own
    feature_count = outgoing.shape[1]
    outgoing = outgoing.reshape(experts, 1, capacity, feature_count)
    outgoing = jnp.broadcast_to(outgoing, (experts, 2, capacity, feature_count)).reshape(
        groups, capacity, feature_count
    )
    whole = lax.all_gather(
        lax.all_to_all(outgoing, "group", split_axis=0, concat_axis=0, tiled=True),
        "tp",
        axis=2,
        tiled=True,
    )
    sources, slot_count, features = whole.shape
    flat_rows = whole.reshape(sources * slot_count, features)
    both = jnp.dot(flat_rows, gate_and_up, preferred_element_type=jnp.float32)
    gate_val = both[:, :hidden_part]
    up_val = both[:, hidden_part:]
    active = (gate_val * jax.nn.sigmoid(ALPHA * gate_val) * (up_val + 1.0)).astype(jnp.bfloat16)
    joined = lax.all_gather(active, "tp", axis=1, tiled=True)
    result = jnp.dot(joined, expert_down[0], preferred_element_type=jnp.float32).astype(
        jnp.bfloat16
    )
    returned = result.reshape(sources, slot_count, result.shape[1])
    arrived = lax.all_to_all(returned, "group", split_axis=0, concat_axis=0, tiled=True)
    halves = arrived.reshape(experts, 2, capacity, width).astype(jnp.float32)
    summed = (halves[:, 0] + halves[:, 1]).reshape(experts * capacity, width)
    rank_at = jnp.take_along_axis(slot_rank, routes, axis=1)
    picked = jnp.take(summed, (routes * capacity + rank_at).reshape(-1), axis=0).reshape(
        block_len, top_count, width
    )
    mixing = route_weights / jnp.sum(route_weights, axis=1, keepdims=True)
    moe_out = jnp.sum(mixing[:, :, None] * picked, axis=1)
    return (own_state + moe_out).astype(jnp.bfloat16)


def solution(mesh):
    return jax.shard_map(
        on_device,
        mesh=mesh,
        in_specs=(
            P("group", "tp"),
            P("group", "tp"),
            P("group", "tp"),
            P("group", "tp"),
            P("group", None),
            P("group"),
            P("tp"),
            P("tp", None),
            P("group", "tp"),
            P(),
            P("group", None),
            P("group", None),
            P("group", None, "tp"),
            P("group", None, "tp"),
            P("group", None, "tp"),
        ),
        out_specs=P("group", "tp"),
        check_vma=False,
    )
```

profile of v0, /device:TPU:0, one launch (start us, length us, event | category | flops | bytes accessed | tf_op | source)
XLA Modules:
  0.0 392.9 jit_solution(7794970646636659135)
XLA Ops:
  6.5 7.5 %all-to-all-start = ((bf16[16,8,512]{2,1,0:T(8,128)(2,1)}), bf16[16,8,512]{2,1,0:T(8,128)(2,1)S(1)}, u32[]{:S(2)}, u32[]{:S(2)}) async-start(bf16[16,8,512]{2,1,0:T(8,128)(2,1)} %bitcast.101), calls=%async_computation | async-start | bytes 262144 | tf_op jit(solution)/shard_map/all_to_all | solution.py:98
  14.8 1.0 reshape.375
  16.4 1.1 reshape.390
  18.1 0.3 fusion.49
  20.0 2.0 all-to-all-done
  24.2 0.3 fusion.75
  26.0 4.6 %fusion.40 = f32[64,2880]{1,0:T(8,128)S(1)} fusion(bf16[1024,2880]{0,1:T(8,128)(2,1)} %param.22, bf16[64,256]{1,0:T(8,128)(2,1)S(1)} %reshape.382, bf16[64,256]{1,0:T(8,128)(2,1)S(1)} %reshape.380, bf16[64,256]{1,0:T(8,128)(2,1)S(1)} %reshape.378, bf16[64,256]{1,0:T(8,128)(2,1)S(1)} %reshape.376), kind=kOutput, calls=%fused_computation.79 | convolution fusion | flops 378011648 | bytes 6766592 | tf_op jit(solution)/shard_map/dot_general | solution.py:117
  30.8 2.1 dynamic_update_slice.3
  32.9 0.9 copy-done
  33.9 0.4 select_reduce_fusion
  34.4 31.8 %all-reduce.3.cloned.1.call-done = f32[64,2880]{1,0:T(8,128)} async-done(((f32[64,2880]{1,0:T(8,128)}), f32[64,2880]{1,0:T(8,128)}) %all-reduce.3.cloned.1.call-update) | async-done | bytes 737296 | tf_op jit(solution)/shard_map/psum | solution.py:120
  66.2 1.3 multiply_reduce_fusion.1
  67.5 1.2 multiply_convert_fusion
  68.7 2.2 gather_fusion
  71.3 50.5 %all_to_all.15 = bf16[16,40,1440]{2,1,0:T(8,128)(2,1)S(1)} all-to-all(bf16[16,40,1440]{2,1,0:T(8,128)(2,1)S(1)} %bitcast.88), channel_id=1, replica_groups=mesh['group'=16,'tp'=2] {'group'}, dimensions={0} | all-to-all | bytes 3686400 | tf_op jit(solution)/shard_map/all_to_all | solution.py:149
  121.7 6.5 %copy.239 = bf16[16,40,1440]{1,0,2:T(8,128)(2,1)} copy(bf16[16,40,1440]{2,1,0:T(8,128)(2,1)S(1)} %all_to_all.15) | data formatting | bytes 3686400 | tf_op jit(solution)/shard_map/all_to_all | solution.py:149
  128.5 142.7 %all-gather.3.cloned.1.call-done = bf16[16,40,2880]{1,0,2:T(8,128)(2,1)} async-done(((bf16[16,40,1440]{1,0,2:T(8,128)(2,1)}), bf16[16,40,2880]{1,0,2:T(8,128)(2,1)}) %all-gather.3.cloned.1.call-update) | async-done | bytes 3686416 | tf_op jit(solution)/shard_map/all_gather | solution.py:148
  271.2 13.3 %copy.240 = bf16[16,40,2880]{2,1,0:T(8,128)(2,1)} copy(bf16[16,40,2880]{1,0,2:T(8,128)(2,1)} %all-gather.3.cloned.1.call-done) | data formatting | bytes 7372800 | tf_op jit(solution)/shard_map/all_gather | solution.py:148
  284.5 11.4 %fusion = f32[640,1440]{0,1:T(8,128)S(1)} fusion(bf16[640,2880]{1,0:T(8,128)(2,1)} %bitcast.91, bf16[2880,720]{0,1:T(8,128)(2,1)} %bitcast.103, bf16[2880,720]{0,1:T(8,128)(2,1)} %bitcast.104), kind=kOutput, calls=%fused_computation.3 | convolution fusion | flops 5325004800 | bytes 15667200 | tf_op jit(solution)/shard_map/dot_general | solution.py:156
  296.0 1.5 fusion.11
  297.5 30.4 %all-gather.5.cloned.1.call-done = bf16[640,1440]{0,1:T(8,128)(2,1)} async-done(((bf16[640,720]{0,1:T(8,128)(2,1)}), bf16[640,1440]{0,1:T(8,128)(2,1)}) %all-gather.5.cloned.1.call-update) | async-done | bytes 1843216 | tf_op jit(solution)/shard_map/all_gather | solution.py:160
  327.9 6.5 %fusion.6 = bf16[640,1440]{0,1:T(8,128)(2,1)S(1)} fusion(bf16[640,1440]{0,1:T(8,128)(2,1)} %all-gather.5.cloned.1.call-done, bf16[1,1440,1440]{2,1,0:T(8,128)(2,1)} %param.29), kind=kOutput, calls=%fused_computation.9 | convolution fusion | flops 2655129600 | bytes 7833600 | tf_op jit(solution)/shard_map/dot_general | solution.py:161
  334.4 2.4 copy.241
  336.8 5.6 %all-to-all-start.2 = ((bf16[16,40,1440]{2,1,0:T(8,128)(2,1)}), bf16[16,40,1440]{2,1,0:T(8,128)(2,1)S(1)}, u32[]{:S(2)}, u32[]{:S(2)}) async-start(bf16[16,40,1440]{2,1,0:T(8,128)(2,1)} %bitcast.89), calls=%async_computation.2 | async-start | bytes 3932160 | tf_op jit(solution)/shard_map/all_to_all | solution.py:165
  342.7 1.9 gather_fusion.2
  345.2 0.7 copy.232
  345.9 35.3 %all-to-all-done.2 = bf16[16,40,1440]{2,1,0:T(8,128)(2,1)S(1)} async-done(((bf16[16,40,1440]{2,1,0:T(8,128)(2,1)}), bf16[16,40,1440]{2,1,0:T(8,128)(2,1)S(1)}, u32[]{:S(2)}, u32[]{:S(2)}) %all-to-all-start.2) | async-done | bytes 1843232 | tf_op jit(solution)/shard_map/all_to_all | solution.py:165
  381.2 0.5 convert.20
  382.0 1.2 gather_fusion.1
  383.3 0.5 gather.20
  384.1 1.4 multiply_reduce_fusion
  385.5 0.9 add_convert_fusion.1
  (117 shorter events, 8.6 us)
Async XLA Ops:
  6.5 11.0 %copy-start.9 = (s32[1,16]{1,0:T(1,128)S(1)}, s32[1,16]{1,0:T(1,128)}, u32[]{:S(2)}) copy-start(s32[1,16]{1,0:T(1,128)} %param.19) | copy-start | bytes 196
  6.5 11.2 %copy-start.7 = (f32[16]{0:T(128)S(1)}, f32[16]{0:T(128)}, u32[]{:S(2)}) copy-start(f32[16]{0:T(128)} %param.21) | copy-start | bytes 196
  6.5 15.5 %all-to-all-start = ((bf16[16,8,512]{2,1,0:T(8,128)(2,1)}), bf16[16,8,512]{2,1,0:T(8,128)(2,1)S(1)}, u32[]{:S(2)}, u32[]{:S(2)}) async-start(bf16[16,8,512]{2,1,0:T(8,128)(2,1)} %bitcast.101), calls=%async_computation | async-start | bytes 262144 | tf_op jit(solution)/shard_map/all_to_all | solution.py:98
  14.1 52.1 %all-reduce.3.cloned.1.call-start = ((), (), s32[]{:S(2)}) async-start(), calls=%async_computation.3 | async-start | bytes 1507328 | tf_op jit(solution)/shard_map/psum | solution.py:120
  16.0 2.4 copy-start.5
  16.0 2.4 copy-start.2
  17.8 2.1 copy-start.8
  26.0 4.6 %copy-start.3 = (bf16[64,1440]{1,0:T(8,128)(2,1)S(1)}, bf16[64,1440]{1,0:T(8,128)(2,1)}, u32[]{:S(2)}) copy-start(bf16[64,1440]{1,0:T(8,128)(2,1)} %param.23) | copy-start | bytes 552964
  32.9 0.9 copy-start
  33.8 237.5 %all-gather.3.cloned.1.call-start = ((), (), s32[]{:S(2)}) async-start(), calls=%async_computation.4 | async-start | bytes 17694720 | tf_op jit(solution)/shard_map/all_gather | solution.py:148
  128.3 199.6 %all-gather.5.cloned.1.call-start = ((), (), s32[]{:S(2)}) async-start(), calls=%async_computation.5 | async-start | bytes 2764800 | tf_op jit(solution)/shard_map/all_gather | solution.py:160
  336.8 44.5 %all-to-all-start.2 = ((bf16[16,40,1440]{2,1,0:T(8,128)(2,1)}), bf16[16,40,1440]{2,1,0:T(8,128)(2,1)S(1)}, u32[]{:S(2)}, u32[]{:S(2)}) async-start(bf16[16,40,1440]{2,1,0:T(8,128)(2,1)} %bitcast.89), calls=%async_computation.2 | async-start | bytes 3932160 | tf_op jit(solution)/shard_map/all_to_all | solution.py:165
  342.6 2.5 copy-start.6
  383.3 0.8 copy-start.4
  384.1 1.5 copy-start.1
Sparse Core Ops, SparseCore 0:
  33.9 32.2 all-reduce.2
  128.4 142.8 all-gather.2
  297.6 30.2 all-gather.4
where the time goes:
time: 399 us; the launch traced here: 393 us
  waiting for transfers between devices  242 us (61%)
  blocking collectives  50.5 us (13%)
  local copies, waits for them, and re-layouts  38.5 us (10%)
  matrix products  24.5 us (6%)
  between operations  14.4 us (4%)
  starting transfers between devices  13.5 us (3%)
  other arithmetic  9.37 us (2%)
    all_gather x1, waiting for transfers between devices, on_device(): lax.all_gather(lax.all_to_all(outgoing, 'group', split_axis=0, concat_axi...  143 us
    all_to_all x1, blocking collectives, on_device(): lax.all_to_all(outgoing, 'group', split_axis=0, concat_axis=0, tiled=True)  50.5 us
    all_to_all x1, waiting for transfers between devices, on_device(): lax.all_to_all(returned, 'group', split_axis=0, concat_axis=0, tiled=True)  35.3 us
    psum x1, waiting for transfers between devices, on_device(): hidden_state = lax.psum(partial_sum, 'tp')  31.8 us
    all_gather x1, waiting for transfers between devices, on_device(): joined = lax.all_gather(active, 'tp', axis=1, tiled=True)  30.4 us
    all_gather x1, local copies, waits for them, and re-layouts, on_device(): lax.all_gather(lax.all_to_all(outgoing, 'group', split_axis=0, concat_axi...  13.3 us
    dot_general x1, matrix products, on_device(): both = jnp.dot(flat_rows, gate_and_up, preferred_element_type=jnp.float32)  11.4 us
  transfers between devices with their start and end apart: 5, of which 5 were waited for; matrix products, arithmetic and copies ran while one was open for 2% of the time, Pallas kernels for 0%

commit v1 on v0

--- a/solution.py
+++ b/solution.py
@@ -1,9 +1,15 @@
+import functools
+
 import jax
 import jax.numpy as jnp
 from jax import lax
+from jax.experimental import pallas as pl
+from jax.experimental.pallas import tpu as pltpu
 from jax.sharding import PartitionSpec as P
 
 HEAD = 64
+CHUNKS = 2
+VMEM_LIMIT = 56 * 1024 * 1024
 
 
 THETA = 150000.0
@@ -75,6 +81,57 @@
     return jnp.concatenate(outputs, axis=1)
 
 
+def exchange(value, axis, offset):
+    if offset == 0:
+        return value
+    size = lax.axis_size(axis)
+    return lax.ppermute(value, axis, [(i, i ^ offset) for i in range(size)])
+
+
+def gate_up_kernel(parts, me_ref, gain_ref, gate_ref, up_ref, *refs):
+    out_ref = refs[-1]
+    rows = refs[0].shape[0]
+    features = gate_ref.shape[0] * gate_ref.shape[1]
+    me = me_ref[0]
+    for s in range(len(refs[:-1]) // parts):
+        held = [refs[s * parts + j][...].astype(jnp.float32) for j in range(parts)]
+        square = sum(jnp.sum(h * h, axis=1, keepdims=True) for h in held)
+        scale = lax.rsqrt(square / features + EPSILON)
+        gate_val = up_val = None
+        for j in range(parts):
+            place = me ^ j
+            normed = (held[j] * scale * gain_ref[place]).astype(jnp.bfloat16)
+            g = jnp.dot(normed, gate_ref[place], preferred_element_type=jnp.float32)
+            u = jnp.dot(normed, up_ref[place], preferred_element_type=jnp.float32)
+            gate_val = g if gate_val is None else gate_val + g
+            up_val = u if up_val is None else up_val + u
+        active = gate_val * jax.nn.sigmoid(ALPHA * gate_val) * (up_val + 1.0)
+        out_ref[pl.ds(s * rows, rows), :] = active.astype(jnp.bfloat16)
+
+
+def down_kernel(me_ref, down_ref, *refs):
+    own_ref, other_ref = refs[-2:]
+    rows = own_ref.shape[0]
+    me = me_ref[0]
+    total = None
+    for j, ref in enumerate(refs[:-2]):
+        term = jnp.dot(ref[...], down_ref[me ^ j], preferred_element_type=jnp.float32)
+        total = term if total is None else total + term
+    own_ref[...] = total[:rows].astype(jnp.bfloat16)
+    other_ref[...] = total[rows:].astype(jnp.bfloat16)
+
+
+def vmem_call(kernel, out_shape, scalar, *operands):
+    return pl.pallas_call(
+        kernel,
+        out_shape=out_shape,
+        in_specs=[pl.BlockSpec(memory_space=pltpu.SMEM)]
+        + [pl.BlockSpec(memory_space=pltpu.VMEM)] * len(operands),
+        out_specs=jax.tree.map(lambda _: pl.BlockSpec(memory_space=pltpu.VMEM), out_shape),
+        compiler_params=pltpu.CompilerParams(vmem_limit_bytes=VMEM_LIMIT),
+    )(scalar, *operands)
+
+
 def on_device(
     queries,
     new_kv,
@@ -93,6 +150,11 @@
     expert_down,
 ):
     groups = lax.axis_size("group")
+    tp = lax.axis_size("tp")
+    me_tp = lax.axis_index("tp")
+    experts = groups // 2
+    me_expert = lax.axis_index("group") // 2
+    tp_scalar = me_tp.astype(jnp.int32).reshape(1)
     lane_count = remote_pool.shape[1]
     local_len = local_cache.shape[0]
     fetched = lax.all_to_all(
@@ -111,66 +173,73 @@
     )
     cache_kv = jnp.concatenate([local_cache, fetched.reshape(-1, lane_count)], axis=0)
     attended = attend(queries, new_kv, cache_kv, cache_valid, sinks, length)
-    width = residual.shape[1]
-    start = lax.axis_index("tp") * width
-    own_gain = lax.dynamic_slice_in_dim(norm_gain, start, width, 0)
+    block_len, width = residual.shape
     partial_sum = jnp.dot(attended, out_weight, preferred_element_type=jnp.float32)
-    own_cols = lax.dynamic_slice_in_dim(partial_sum, start, width, 1) + residual.astype(jnp.float32)
-    partial_sum = lax.dynamic_update_slice_in_dim(partial_sum, own_cols, start, 1)
-    hidden_state = lax.psum(partial_sum, "tp")
-    mean_square = jnp.mean(hidden_state * hidden_state, axis=1, keepdims=True)
-    own_state = lax.dynamic_slice_in_dim(hidden_state, start, width, 1)
-    normed_own = (own_state * lax.rsqrt(mean_square + EPSILON) * own_gain).astype(jnp.bfloat16)
-    block_len = normed_own.shape[0]
+
+    def columns(place):
+        return lax.dynamic_slice_in_dim(partial_sum, place * width, width, 1)
+
+    own_state = columns(me_tp) + residual.astype(jnp.float32)
+    for j in range(1, tp):
+        own_state = own_state + exchange(
+            columns(me_tp ^ j).astype(jnp.bfloat16), "tp", j
+        ).astype(jnp.float32)
+    state_sent = own_state.astype(jnp.bfloat16)
+
     top_count = routes.shape[1]
-    experts = groups // 2
     capacity = 5 * block_len * top_count // (4 * experts)
-    member = jnp.any(
-        routes[:, :, None] == jnp.arange(experts, dtype=jnp.int32)[None, None, :], axis=1
+    mixing = route_weights / jnp.sum(route_weights, axis=1, keepdims=True)
+    chosen = (routes ^ me_expert)[:, :, None] == jnp.arange(experts, dtype=jnp.int32)
+    member = jnp.any(chosen, axis=1)
+    mix = jnp.sum(jnp.where(chosen, mixing[:, :, None], 0.0), axis=1)
+    earlier = jnp.arange(block_len)[:, None] > jnp.arange(block_len)[None, :]
+    rank = jnp.dot(
+        earlier.astype(jnp.bfloat16), member.astype(jnp.bfloat16), preferred_element_type=jnp.float32
     ).astype(jnp.int32)
-    slot_rank = jnp.cumsum(member, axis=0) - member
-    slot_hit = member[:, :, None] * (
-        slot_rank[:, :, None] == jnp.arange(capacity, dtype=jnp.int32)[None, None, :]
-    ).astype(jnp.int32)
-    slot_token = jnp.sum(slot_hit * jnp.arange(block_len, dtype=jnp.int32)[:, None, None], axis=0)
-    slot_valid = jnp.sum(slot_hit, axis=0)
-    send_own = jnp.take(normed_own, slot_token.reshape(-1), axis=0) * slot_valid.reshape(
-        -1, 1
-    ).astype(jnp.bfloat16)
-    hidden_part = expert_gate.shape[2]
-    gate_and_up = jnp.concatenate([expert_gate[0], expert_up[0]], axis=1)
-    outgoing = send_own
-    feature_count = outgoing.shape[1]
-    outgoing = outgoing.reshape(experts, 1, capacity, feature_count)
-    outgoing = jnp.broadcast_to(outgoing, (experts, 2, capacity, feature_count)).reshape(
-        groups, capacity, feature_count
-    )
-    whole = lax.all_gather(
-        lax.all_to_all(outgoing, "group", split_axis=0, concat_axis=0, tiled=True),
-        "tp",
-        axis=2,
-        tiled=True,
-    )
-    sources, slot_count, features = whole.shape
-    flat_rows = whole.reshape(sources * slot_count, features)
-    both = jnp.dot(flat_rows, gate_and_up, preferred_element_type=jnp.float32)
-    gate_val = both[:, :hidden_part]
-    up_val = both[:, hidden_part:]
-    active = (gate_val * jax.nn.sigmoid(ALPHA * gate_val) * (up_val + 1.0)).astype(jnp.bfloat16)
-    joined = lax.all_gather(active, "tp", axis=1, tiled=True)
-    result = jnp.dot(joined, expert_down[0], preferred_element_type=jnp.float32).astype(
-        jnp.bfloat16
-    )
-    returned = result.reshape(sources, slot_count, result.shape[1])
-    arrived = lax.all_to_all(returned, "group", split_axis=0, concat_axis=0, tiled=True)
-    halves = arrived.reshape(experts, 2, capacity, width).astype(jnp.float32)
-    summed = (halves[:, 0] + halves[:, 1]).reshape(experts * capacity, width)
-    rank_at = jnp.take_along_axis(slot_rank, routes, axis=1)
-    picked = jnp.take(summed, (routes * capacity + rank_at).reshape(-1), axis=0).reshape(
-        block_len, top_count, width
-    )
-    mixing = route_weights / jnp.sum(route_weights, axis=1, keepdims=True)
-    moe_out = jnp.sum(mixing[:, :, None] * picked, axis=1)
+    hit = member.T[:, None, :] & (
+        rank.T[:, None, :] == jnp.arange(capacity, dtype=jnp.int32)[None, :, None]
+    )
+    pick = hit.astype(jnp.bfloat16).reshape(experts * capacity, block_len)
+    spread = jnp.where(hit, mix.T[:, None, :], 0.0).reshape(experts * capacity, block_len)
+    spread_high = spread.astype(jnp.bfloat16)
+    spread_low = (spread - spread_high.astype(jnp.float32)).astype(jnp.bfloat16)
+
+    send = jnp.dot(pick, state_sent, preferred_element_type=jnp.float32).astype(jnp.bfloat16)
+    send = send.reshape(experts, capacity, width)
+    hidden = expert_gate.shape[2]
+    gate = expert_gate.reshape(tp, width, hidden)
+    up = expert_up.reshape(tp, width, hidden)
+    down = expert_down.reshape(tp, hidden, width)
+    gain = norm_gain.reshape(tp, 1, width)
+    per_chunk = experts // CHUNKS
+    rows = per_chunk * capacity
+    back = []
+    for c in range(CHUNKS):
+        steps = range(c * per_chunk, (c + 1) * per_chunk)
+        held = jnp.concatenate([exchange(send[d], "group", 2 * d) for d in steps], axis=0)
+        blocks = [exchange(held, "tp", j) for j in range(tp)]
+        others = [exchange(block, "group", 1) for block in blocks]
+        active = vmem_call(
+            functools.partial(gate_up_kernel, tp),
+            jax.ShapeDtypeStruct((2 * rows, hidden), jnp.bfloat16),
+            tp_scalar,
+            gain,
+            gate,
+            up,
+            *blocks,
+            *others,
+        )
+        actives = [exchange(active, "tp", j) for j in range(tp)]
+        out_type = jax.ShapeDtypeStruct((rows, width), jnp.bfloat16)
+        mine, theirs = vmem_call(down_kernel, [out_type, out_type], tp_scalar, down, *actives)
+        summed = mine.astype(jnp.float32) + exchange(theirs, "group", 1).astype(jnp.float32)
+        summed = summed.astype(jnp.bfloat16).reshape(per_chunk, capacity, width)
+        back += [exchange(summed[i], "group", 2 * d) for i, d in enumerate(steps)]
+    returned = jnp.concatenate(back, axis=0)
+    rows_first = (((0,), (0,)), ((), ()))
+    moe_out = lax.dot_general(
+        spread_high, returned, rows_first, preferred_element_type=jnp.float32
+    ) + lax.dot_general(spread_low, returned, rows_first, preferred_element_type=jnp.float32)
     return (own_state + moe_out).astype(jnp.bfloat16)
 
 

time: 399 us -> 141 us (0.35); the launches traced: 393 us -> 139 us
  waiting for transfers between devices: 242 us -> 37.6 us
  blocking collectives: 50.5 us -> 0 us
  Pallas kernels: 0 us -> 27.5 us
  starting transfers between devices: 13.5 us -> 37.2 us
  matrix products: 24.5 us -> 8.59 us
  local copies, waits for them, and re-layouts: 38.5 us -> 23.3 us
  between operations: 14.4 us -> 1.25 us
  other arithmetic: 9.37 us -> 3.76 us
    all_gather x2 -> x0, waiting for transfers between devices: 173 us -> none  [the longest x1 143 us: on_device(): lax.all_gather(lax.all_to_all(outgoing, 'group', split_axis=0, concat_axi...]
    all_to_all x1 -> x0, blocking collectives: 50.5 us -> none  [on_device(): lax.all_to_all(outgoing, 'group', split_axis=0, concat_axis=0, tiled=True)]
    ppermute x0 -> x25, waiting for transfers between devices: none -> 36.7 us  [exchange(): return lax.ppermute(value, axis, [(i, i ^ offset) for i in range(size)])]
    all_to_all x1 -> x0, waiting for transfers between devices: 35.3 us -> none  [on_device(): lax.all_to_all(returned, 'group', split_axis=0, concat_axis=0, tiled=True)]
    psum x1 -> x0, waiting for transfers between devices: 31.8 us -> none  [on_device(): hidden_state = lax.psum(partial_sum, 'tp')]
    ppermute x0 -> x25, starting transfers between devices: none -> 29.6 us  [exchange(): return lax.ppermute(value, axis, [(i, i ^ offset) for i in range(size)])]
    pallas_call x0 -> x4, Pallas kernels: none -> 27.5 us  [vmem_call(): pl.pallas_call(kernel, out_shape=out_shape, in_specs=[pl.BlockSpec(memory...]
    dot_general x2 -> x4, matrix products: 17.9 us -> 2.03 us  [the longest x1 1.06 us: on_device(): lax.dot_general(spread_high, returned, rows_first, preferred_element_type...]
  transfers between devices with their start and end apart: 5 -> 26, of which waited for: 5 -> 11; matrix products, arithmetic and copies ran while one was open for 2% -> 16% of each run, Pallas kernels for 0% -> 20%
where the time goes in v1:
time: 141 us; the launch traced here: 139 us
  waiting for transfers between devices  37.6 us (27%)
  starting transfers between devices  37.2 us (26%)
  Pallas kernels  27.5 us (20%)
  local copies, waits for them, and re-layouts  23.3 us (17%)
  matrix products  8.59 us (6%)
  other arithmetic  3.76 us (3%)
    ppermute x25, waiting for transfers between devices, exchange(): return lax.ppermute(value, axis, [(i, i ^ offset) for i in range(size)])  36.7 us
    ppermute x25, starting transfers between devices, exchange(): return lax.ppermute(value, axis, [(i, i ^ offset) for i in range(size)])  29.6 us
    pallas_call x4, Pallas kernels, vmem_call(): pl.pallas_call(kernel, out_shape=out_shape, in_specs=[pl.BlockSpec(memory...  27.5 us
    unnamed x41, local copies, waits for them, and re-layouts  16.6 us
    all_to_all x1, starting transfers between devices, on_device(): lax.all_to_all(remote_pool.reshape(groups, -1, lane_count), 'group', spli...  7.52 us
    dot_general x1, matrix products, on_device(): jnp.dot(attended, out_weight, preferred_element_type=jnp.float32)  4.58 us
  transfers between devices with their start and end apart: 26, of which 11 were waited for; matrix products, arithmetic and copies ran while one was open for 16% of the time, Pallas kernels for 20%

profile of v1, /device:TPU:0, one launch (start us, length us, event | category | flops | bytes accessed | tf_op | source)
XLA Modules:
  0.0 139.1 jit_solution(16696450293662626338)
XLA Ops:
  0.0 7.5 %all-to-all-start = ((bf16[16,8,512]{2,1,0:T(8,128)(2,1)}), bf16[16,8,512]{2,1,0:T(8,128)(2,1)S(1)}, u32[]{:S(2)}, u32[]{:S(2)}) async-start(bf16[16,8,512]{2,1,0:T(8,128)(2,1)} %bitcast.108), calls=%async_computation | async-start | bytes 262144 | tf_op jit(solution)/shard_map/all_to_all | solution.py:160
  9.8 1.1 reshape.302
  19.4 4.6 %fusion.34 = f32[64,2880]{1,0:T(8,128)S(1)} fusion(bf16[1024,2880]{0,1:T(8,128)(2,1)} %param.22, bf16[64,256]{1,0:T(8,128)(2,1)S(1)} %reshape.295, bf16[64,256]{1,0:T(8,128)(2,1)S(1)} %reshape.293, bf16[64,256]{1,0:T(8,128)(2,1)S(1)} %reshape.291, bf16[64,256]{1,0:T(8,128)(2,1)S(1)} %reshape.289), kind=kOutput, calls=%fused_computation.70 | convolution fusion | flops 378011648 | bytes 6766592 | tf_op jit(solution)/shard_map/dot_general | solution.py:177
  24.2 1.6 %collective-permute-start = (bf16[64,1440]{1,0:T(8,128)(2,1)S(1)}, bf16[64,1440]{1,0:T(8,128)(2,1)S(1)}, u32[]{:S(2)}, u32[]{:S(2)}) collective-permute-start(bf16[64,1440]{1,0:T(8,128)(2,1)S(1)} %dynamic-slice_convert_fusion), channel_id=1, source_target_pairs={{0,1},{1,0},{2,3},{3,2},{4,5},{5,4},{6,7},{7,6},{8,9},{9,8},{10,11... | collective-permute-start | bytes 552968 | tf_op jit(solution)/shard_map/ppermute | solution.py:88
  26.0 4.6 %collective-permute-done = bf16[64,1440]{1,0:T(8,128)(2,1)S(1)} collective-permute-done((bf16[64,1440]{1,0:T(8,128)(2,1)S(1)}, bf16[64,1440]{1,0:T(8,128)(2,1)S(1)}, u32[]{:S(2)}, u32[]{:S(2)}) %collective-permute-start) | collective-permute-done | bytes 184352 | tf_op jit(solution)/shard_map/ppermute | solution.py:88
  31.2 1.7 %collective-permute-start.1 = (bf16[40,1440]{1,0:T(8,128)(2,1)S(1)}, bf16[40,1440]{1,0:T(8,128)(2,1)S(1)}, u32[]{:S(2)}, u32[]{:S(2)}) collective-permute-start(bf16[40,1440]{1,0:T(8,128)(2,1)S(1)} %get-tuple-element.19), channel_id=1, source_target_pairs={{0,4},{2,6},{4,0},{6,2},{8,12},{10,14},{12,8},{14,10},{16,20},{18,... | collective-permute-start | bytes 345608 | tf_op jit(solution)/shard_map/ppermute | solution.py:88
  32.9 1.5 %collective-permute-start.2 = (bf16[40,1440]{1,0:T(8,128)(2,1)S(1)}, bf16[40,1440]{1,0:T(8,128)(2,1)S(1)}, u32[]{:S(2)}, u32[]{:S(2)}) collective-permute-start(bf16[40,1440]{1,0:T(8,128)(2,1)S(1)} %get-tuple-element.18), channel_id=1, source_target_pairs={{0,8},{2,10},{4,12},{6,14},{8,0},{10,2},{12,4},{14,6},{16,24},{18,... | collective-permute-start | bytes 345608 | tf_op jit(solution)/shard_map/ppermute | solution.py:88
  34.7 2.6 %collective-permute-start.12 = (bf16[40,1440]{1,0:T(8,128)(2,1)S(1)}, bf16[40,1440]{1,0:T(8,128)(2,1)S(1)}, u32[]{:S(2)}, u32[]{:S(2)}) collective-permute-start(bf16[40,1440]{1,0:T(8,128)(2,1)S(1)} %get-tuple-element.16), channel_id=1, source_target_pairs={{0,16},{2,18},{4,20},{6,22},{8,24},{10,26},{12,28},{14,30},{16,0},... | collective-permute-start | bytes 345608 | tf_op jit(solution)/shard_map/ppermute | solution.py:88
  37.3 1.5 %collective-permute-start.13 = (bf16[40,1440]{1,0:T(8,128)(2,1)S(1)}, bf16[40,1440]{1,0:T(8,128)(2,1)S(1)}, u32[]{:S(2)}, u32[]{:S(2)}) collective-permute-start(bf16[40,1440]{1,0:T(8,128)(2,1)S(1)} %get-tuple-element.15), channel_id=1, source_target_pairs={{0,20},{2,22},{4,16},{6,18},{8,28},{10,30},{12,24},{14,26},{16,4},... | collective-permute-start | bytes 345608 | tf_op jit(solution)/shard_map/ppermute | solution.py:88
  38.8 3.3 %collective-permute-start.14 = (bf16[40,1440]{1,0:T(8,128)(2,1)S(1)}, bf16[40,1440]{1,0:T(8,128)(2,1)S(1)}, u32[]{:S(2)}, u32[]{:S(2)}) collective-permute-start(bf16[40,1440]{1,0:T(8,128)(2,1)S(1)} %get-tuple-element.14), channel_id=1, source_target_pairs={{0,24},{2,26},{4,28},{6,30},{8,16},{10,18},{12,20},{14,22},{16,8},... | collective-permute-start | bytes 345608 | tf_op jit(solution)/shard_map/ppermute | solution.py:88
  42.5 1.4 collective-permute-done.3
  44.0 1.5 %collective-permute-start.4 = (bf16[160,1440]{1,0:T(8,128)(2,1)S(1)}, bf16[160,1440]{1,0:T(8,128)(2,1)S(1)}, u32[]{:S(2)}, u32[]{:S(2)}) collective-permute-start(bf16[160,1440]{1,0:T(8,128)(2,1)S(1)} %pad_maximum_fusion.refs_0_), channel_id=1, source_target_pairs={{0,1},{1,0},{2,3},{3,2},{4,5},{5,4},{6,7},{7,6},{8,9},{9,8},{10,11... | collective-permute-start | bytes 1382408 | tf_op jit(solution)/shard_map/ppermute | solution.py:88
  45.5 10.5 %collective-permute-done.13 = bf16[40,1440]{1,0:T(8,128)(2,1)S(1)} collective-permute-done((bf16[40,1440]{1,0:T(8,128)(2,1)S(1)}, bf16[40,1440]{1,0:T(8,128)(2,1)S(1)}, u32[]{:S(2)}, u32[]{:S(2)}) %collective-permute-start.13) | collective-permute-done | bytes 115232 | tf_op jit(solution)/shard_map/ppermute | solution.py:88
  56.1 1.6 %collective-permute-start.16 = (bf16[160,1440]{1,0:T(8,128)(2,1)S(1)}, bf16[160,1440]{1,0:T(8,128)(2,1)S(1)}, u32[]{:S(2)}, u32[]{:S(2)}) collective-permute-start(bf16[160,1440]{1,0:T(8,128)(2,1)S(1)} %constant_dynamic-update-slice_fusion.refs_0_), channel_id=1, source_target_pairs={{0,1},{1,0},{2,3},{3,2},{4,5},{5,4},{6,7},{7,6},{8,9},{9,8},{10,11... | collective-permute-start | bytes 1382408 | tf_op jit(solution)/shard_map/ppermute | solution.py:88
  58.2 6.5 %copy.94 = bf16[1,2880,720]{2,1,0:T(8,128)(2,1)} copy(bf16[1,2880,720]{1,2,0:T(8,128)(2,1)} %param.27) | data formatting | bytes 8294400 | tf_op args[12]
  64.8 6.5 %copy.95 = bf16[1,2880,720]{2,1,0:T(8,128)(2,1)} copy(bf16[1,2880,720]{1,2,0:T(8,128)(2,1)} %param.28) | data formatting | bytes 8294400 | tf_op args[13]
  72.5 8.6 %shard_map.145.refs_0_ = bf16[320,720]{1,0:T(8,128)(2,1)} custom-call(s32[1]{0:T(128)} %bitcast.27.me_ref, f32[2,1,1440]{2,1,0:T(1,128)} %reshape.298.gain_ref, bf16[2,1440,720]{2,1,0:T(8,128)(2,1)} %bitcast.93, bf16[2,1440,720]{2,1,0:T(8,128)(2,1)} %bitcast.95, bf16[160,1440]{1,0:T(8,128)(2,1)} %copy-done, bf16[160,1440]{1,0:T(8,128)(2,1)} %copy-done.3, ...), custom_call_target="tpu_custom_call" | custom-call | tf_op jit(solution)/shard_map/pallas_call | solution.py:125
  83.2 8.6 %shard_map.147.refs_0_ = bf16[320,720]{1,0:T(8,128)(2,1)} custom-call(s32[1]{0:T(128)} %bitcast.27.me_ref, f32[2,1,1440]{2,1,0:T(1,128)} %reshape.298.gain_ref, bf16[2,1440,720]{2,1,0:T(8,128)(2,1)} %bitcast.94, bf16[2,1440,720]{2,1,0:T(8,128)(2,1)} %bitcast.96, bf16[160,1440]{1,0:T(8,128)(2,1)} %copy-done.2, bf16[160,1440]{1,0:T(8,128)(2,1)} %copy-done.4, ...), custom_call_target="tpu_custom_call" | custom-call | tf_op jit(solution)/shard_map/pallas_call | solution.py:125
  91.8 1.5 %collective-permute-start.19 = (bf16[320,720]{1,0:T(8,128)(2,1)}, bf16[320,720]{1,0:T(8,128)(2,1)S(1)}, u32[]{:S(2)}, u32[]{:S(2)}) collective-permute-start(bf16[320,720]{1,0:T(8,128)(2,1)} %shard_map.147.refs_0_), channel_id=1, source_target_pairs={{0,1},{1,0},{2,3},{3,2},{4,5},{5,4},{6,7},{7,6},{8,9},{9,8},{10,11... | collective-permute-start | bytes 1382408 | tf_op jit(solution)/shard_map/ppermute | solution.py:88
  93.3 1.4 collective-permute-done.7.refs_1_
  95.5 5.1 %shard_map.146 = (bf16[160,1440]{1,0:T(8,128)(2,1)}, bf16[160,1440]{1,0:T(8,128)(2,1)}) custom-call(s32[1]{0:T(128)} %bitcast.27.me_ref, bf16[2,720,1440]{2,1,0:T(8,128)(2,1)} %bitcast.97, bf16[320,720]{1,0:T(8,128)(2,1)} %shard_map.145.refs_0_, bf16[320,720]{1,0:T(8,128)(2,1)} %copy-done.9), custom_call_target="tpu_custom_call" | custom-call | tf_op jit(solution)/shard_map/pallas_call | solution.py:125
  100.9 4.3 %collective-permute-done.19.refs_1_ = bf16[320,720]{1,0:T(8,128)(2,1)S(1)} collective-permute-done((bf16[320,720]{1,0:T(8,128)(2,1)}, bf16[320,720]{1,0:T(8,128)(2,1)S(1)}, u32[]{:S(2)}, u32[]{:S(2)}) %collective-permute-start.19) | collective-permute-done | bytes 460832 | tf_op jit(solution)/shard_map/ppermute | solution.py:88
  106.0 5.1 %shard_map.148 = (bf16[160,1440]{1,0:T(8,128)(2,1)}, bf16[160,1440]{1,0:T(8,128)(2,1)}) custom-call(s32[1]{0:T(128)} %bitcast.27.me_ref, bf16[2,720,1440]{2,1,0:T(8,128)(2,1)} %bitcast.98, bf16[320,720]{1,0:T(8,128)(2,1)} %shard_map.147.refs_0_, bf16[320,720]{1,0:T(8,128)(2,1)} %copy-done.8), custom_call_target="tpu_custom_call" | custom-call | tf_op jit(solution)/shard_map/pallas_call | solution.py:125
  111.3 1.8 %collective-permute-done.20 = bf16[160,1440]{1,0:T(8,128)(2,1)S(1)} collective-permute-done((bf16[160,1440]{1,0:T(8,128)(2,1)}, bf16[160,1440]{1,0:T(8,128)(2,1)S(1)}, u32[]{:S(2)}, u32[]{:S(2)}) %collective-permute-start.20) | collective-permute-done | bytes 460832 | tf_op jit(solution)/shard_map/ppermute | solution.py:88
  113.2 1.1 add_convert_fusion
  114.3 5.2 %collective-permute-start.21 = (bf16[40,1440]{1,0:T(8,128)(2,1)S(1)}, bf16[40,1440]{1,0:T(8,128)(2,1)S(1)}, u32[]{:S(2)}, u32[]{:S(2)}) collective-permute-start(bf16[40,1440]{1,0:T(8,128)(2,1)S(1)} %get-tuple-element.30), channel_id=1, source_target_pairs={{0,16},{2,18},{4,20},{6,22},{8,24},{10,26},{12,28},{14,30},{16,0},... | collective-permute-start | bytes 345608 | tf_op jit(solution)/shard_map/ppermute | solution.py:88
  119.5 2.0 %collective-permute-start.11 = (bf16[40,1440]{1,0:T(8,128)(2,1)S(1)}, bf16[40,1440]{1,0:T(8,128)(2,1)S(1)}, u32[]{:S(2)}, u32[]{:S(2)}) collective-permute-start(bf16[40,1440]{1,0:T(8,128)(2,1)S(1)} %get-tuple-element.31), channel_id=1, source_target_pairs={{0,12},{2,14},{4,8},{6,10},{8,4},{10,6},{12,0},{14,2},{16,28},{18,... | collective-permute-start | bytes 345608 | tf_op jit(solution)/shard_map/ppermute | solution.py:88
  122.5 2.3 %collective-permute-start.23 = (bf16[40,1440]{1,0:T(8,128)(2,1)S(1)}, bf16[40,1440]{1,0:T(8,128)(2,1)S(1)}, u32[]{:S(2)}, u32[]{:S(2)}) collective-permute-start(bf16[40,1440]{1,0:T(8,128)(2,1)S(1)} %get-tuple-element.28), channel_id=1, source_target_pairs={{0,24},{2,26},{4,28},{6,30},{8,16},{10,18},{12,20},{14,22},{16,8},... | collective-permute-start | bytes 345608 | tf_op jit(solution)/shard_map/ppermute | solution.py:88
  124.8 4.8 %collective-permute-done.10 = bf16[40,1440]{1,0:T(8,128)(2,1)S(1)} collective-permute-done((bf16[40,1440]{1,0:T(8,128)(2,1)S(1)}, bf16[40,1440]{1,0:T(8,128)(2,1)S(1)}, u32[]{:S(2)}, u32[]{:S(2)}) %collective-permute-start.10) | collective-permute-done | bytes 115232 | tf_op jit(solution)/shard_map/ppermute | solution.py:88
  129.7 1.5 %collective-permute-done.11 = bf16[40,1440]{1,0:T(8,128)(2,1)S(1)} collective-permute-done((bf16[40,1440]{1,0:T(8,128)(2,1)S(1)}, bf16[40,1440]{1,0:T(8,128)(2,1)S(1)}, u32[]{:S(2)}, u32[]{:S(2)}) %collective-permute-start.11) | collective-permute-done | bytes 115232 | tf_op jit(solution)/shard_map/ppermute | solution.py:88
  131.2 4.5 %collective-permute-done.23 = bf16[40,1440]{1,0:T(8,128)(2,1)S(1)} collective-permute-done((bf16[40,1440]{1,0:T(8,128)(2,1)S(1)}, bf16[40,1440]{1,0:T(8,128)(2,1)S(1)}, u32[]{:S(2)}, u32[]{:S(2)}) %collective-permute-start.23) | collective-permute-done | bytes 115232 | tf_op jit(solution)/shard_map/ppermute | solution.py:88
  135.7 2.0 %collective-permute-done.24 = bf16[40,1440]{1,0:T(8,128)(2,1)S(1)} collective-permute-done((bf16[40,1440]{1,0:T(8,128)(2,1)S(1)}, bf16[40,1440]{1,0:T(8,128)(2,1)S(1)}, u32[]{:S(2)}, u32[]{:S(2)}) %collective-permute-start.24) | collective-permute-done | bytes 115232 | tf_op jit(solution)/shard_map/ppermute | solution.py:88
  (153 shorter events, 20.2 us)
Async XLA Ops:
  0.0 13.2 %copy-start.13 = (s32[64,4]{0,1:T(4,128)S(1)}, s32[64,4]{0,1:T(4,128)}, u32[]{:S(2)}) copy-start(s32[64,4]{0,1:T(4,128)} %param.25) | copy-start | bytes 3076
  0.0 13.3 %copy-start.10 = (bf16[256,512]{1,0:T(8,128)(2,1)S(1)}, bf16[256,512]{1,0:T(8,128)(2,1)}, u32[]{:S(2)}) copy-start(bf16[256,512]{1,0:T(8,128)(2,1)} %param.17) | copy-start | bytes 786436
  0.0 15.5 %all-to-all-start = ((bf16[16,8,512]{2,1,0:T(8,128)(2,1)}), bf16[16,8,512]{2,1,0:T(8,128)(2,1)S(1)}, u32[]{:S(2)}, u32[]{:S(2)}) async-start(bf16[16,8,512]{2,1,0:T(8,128)(2,1)} %bitcast.108), calls=%async_computation | async-start | bytes 262144 | tf_op jit(solution)/shard_map/all_to_all | solution.py:160
  18.8 11.8 %copy-start.1 = (bf16[64,1440]{1,0:T(8,128)(2,1)S(1)}, bf16[64,1440]{1,0:T(8,128)(2,1)}, u32[]{:S(2)}) copy-start(bf16[64,1440]{1,0:T(8,128)(2,1)} %param.23) | copy-start | bytes 552964
  24.2 6.4 %collective-permute-start = (bf16[64,1440]{1,0:T(8,128)(2,1)S(1)}, bf16[64,1440]{1,0:T(8,128)(2,1)S(1)}, u32[]{:S(2)}, u32[]{:S(2)}) collective-permute-start(bf16[64,1440]{1,0:T(8,128)(2,1)S(1)} %dynamic-slice_convert_fusion), channel_id=1, source_target_pairs={{0,1},{1,0},{2,3},{3,2},{4,5},{5,4},{6,7},{7,6},{8,9},{9,8},{10,11... | collective-permute-start | bytes 552968 | tf_op jit(solution)/shard_map/ppermute | solution.py:88
  31.2 7.6 %collective-permute-start.1 = (bf16[40,1440]{1,0:T(8,128)(2,1)S(1)}, bf16[40,1440]{1,0:T(8,128)(2,1)S(1)}, u32[]{:S(2)}, u32[]{:S(2)}) collective-permute-start(bf16[40,1440]{1,0:T(8,128)(2,1)S(1)} %get-tuple-element.19), channel_id=1, source_target_pairs={{0,4},{2,6},{4,0},{6,2},{8,12},{10,14},{12,8},{14,10},{16,20},{18,... | collective-permute-start | bytes 345608 | tf_op jit(solution)/shard_map/ppermute | solution.py:88
  32.9 9.1 %collective-permute-start.2 = (bf16[40,1440]{1,0:T(8,128)(2,1)S(1)}, bf16[40,1440]{1,0:T(8,128)(2,1)S(1)}, u32[]{:S(2)}, u32[]{:S(2)}) collective-permute-start(bf16[40,1440]{1,0:T(8,128)(2,1)S(1)} %get-tuple-element.18), channel_id=1, source_target_pairs={{0,8},{2,10},{4,12},{6,14},{8,0},{10,2},{12,4},{14,6},{16,24},{18,... | collective-permute-start | bytes 345608 | tf_op jit(solution)/shard_map/ppermute | solution.py:88
  34.4 9.5 %collective-permute-start.3 = (bf16[40,1440]{1,0:T(8,128)(2,1)S(1)}, bf16[40,1440]{1,0:T(8,128)(2,1)S(1)}, u32[]{:S(2)}, u32[]{:S(2)}) collective-permute-start(bf16[40,1440]{1,0:T(8,128)(2,1)S(1)} %get-tuple-element.17), channel_id=1, source_target_pairs={{0,12},{2,14},{4,8},{6,10},{8,4},{10,6},{12,0},{14,2},{16,28},{18,... | collective-permute-start | bytes 345608 | tf_op jit(solution)/shard_map/ppermute | solution.py:88
  34.7 10.8 %collective-permute-start.12 = (bf16[40,1440]{1,0:T(8,128)(2,1)S(1)}, bf16[40,1440]{1,0:T(8,128)(2,1)S(1)}, u32[]{:S(2)}, u32[]{:S(2)}) collective-permute-start(bf16[40,1440]{1,0:T(8,128)(2,1)S(1)} %get-tuple-element.16), channel_id=1, source_target_pairs={{0,16},{2,18},{4,20},{6,22},{8,24},{10,26},{12,28},{14,30},{16,0},... | collective-permute-start | bytes 345608 | tf_op jit(solution)/shard_map/ppermute | solution.py:88
  37.3 18.8 %collective-permute-start.13 = (bf16[40,1440]{1,0:T(8,128)(2,1)S(1)}, bf16[40,1440]{1,0:T(8,128)(2,1)S(1)}, u32[]{:S(2)}, u32[]{:S(2)}) collective-permute-start(bf16[40,1440]{1,0:T(8,128)(2,1)S(1)} %get-tuple-element.15), channel_id=1, source_target_pairs={{0,20},{2,22},{4,16},{6,18},{8,28},{10,30},{12,24},{14,26},{16,4},... | collective-permute-start | bytes 345608 | tf_op jit(solution)/shard_map/ppermute | solution.py:88
  38.8 17.3 %collective-permute-start.14 = (bf16[40,1440]{1,0:T(8,128)(2,1)S(1)}, bf16[40,1440]{1,0:T(8,128)(2,1)S(1)}, u32[]{:S(2)}, u32[]{:S(2)}) collective-permute-start(bf16[40,1440]{1,0:T(8,128)(2,1)S(1)} %get-tuple-element.14), channel_id=1, source_target_pairs={{0,24},{2,26},{4,28},{6,30},{8,16},{10,18},{12,20},{14,22},{16,8},... | collective-permute-start | bytes 345608 | tf_op jit(solution)/shard_map/ppermute | solution.py:88
  42.0 14.1 %collective-permute-start.15 = (bf16[40,1440]{1,0:T(8,128)(2,1)S(1)}, bf16[40,1440]{1,0:T(8,128)(2,1)S(1)}, u32[]{:S(2)}, u32[]{:S(2)}) collective-permute-start(bf16[40,1440]{1,0:T(8,128)(2,1)S(1)} %get-tuple-element.13), channel_id=1, source_target_pairs={{0,28},{2,30},{4,24},{6,26},{8,20},{10,22},{12,16},{14,18},{16,12}... | collective-permute-start | bytes 345608 | tf_op jit(solution)/shard_map/ppermute | solution.py:88
  44.0 20.8 %copy-start = (bf16[160,1440]{1,0:T(8,128)(2,1)}, bf16[160,1440]{1,0:T(8,128)(2,1)S(1)}, u32[]{:S(2)}) copy-start(bf16[160,1440]{1,0:T(8,128)(2,1)S(1)} %pad_maximum_fusion.refs_0_) | copy-start | bytes 1382404
  44.0 13.8 %collective-permute-start.4 = (bf16[160,1440]{1,0:T(8,128)(2,1)S(1)}, bf16[160,1440]{1,0:T(8,128)(2,1)S(1)}, u32[]{:S(2)}, u32[]{:S(2)}) collective-permute-start(bf16[160,1440]{1,0:T(8,128)(2,1)S(1)} %pad_maximum_fusion.refs_0_), channel_id=1, source_target_pairs={{0,1},{1,0},{2,3},{3,2},{4,5},{5,4},{6,7},{7,6},{8,9},{9,8},{10,11... | collective-permute-start | bytes 1382408 | tf_op jit(solution)/shard_map/ppermute | solution.py:88
  56.1 15.8 %copy-start.2 = (bf16[160,1440]{1,0:T(8,128)(2,1)}, bf16[160,1440]{1,0:T(8,128)(2,1)S(1)}, u32[]{:S(2)}) copy-start(bf16[160,1440]{1,0:T(8,128)(2,1)S(1)} %constant_dynamic-update-slice_fusion.refs_0_) | copy-start | bytes 1382404
  56.1 16.0 %collective-permute-start.16 = (bf16[160,1440]{1,0:T(8,128)(2,1)S(1)}, bf16[160,1440]{1,0:T(8,128)(2,1)S(1)}, u32[]{:S(2)}, u32[]{:S(2)}) collective-permute-start(bf16[160,1440]{1,0:T(8,128)(2,1)S(1)} %constant_dynamic-update-slice_fusion.refs_0_), channel_id=1, source_target_pairs={{0,1},{1,0},{2,3},{3,2},{4,5},{5,4},{6,7},{7,6},{8,9},{9,8},{10,11... | collective-permute-start | bytes 1382408 | tf_op jit(solution)/shard_map/ppermute | solution.py:88
  57.7 14.8 %collective-permute-start.5 = (bf16[160,1440]{1,0:T(8,128)(2,1)S(1)}, bf16[160,1440]{1,0:T(8,128)(2,1)}, u32[]{:S(2)}, u32[]{:S(2)}) collective-permute-start(bf16[160,1440]{1,0:T(8,128)(2,1)S(1)} %pad_maximum_fusion.refs_0_), channel_id=1, source_target_pairs={{0,2},{2,0},{4,6},{6,4},{8,10},{10,8},{12,14},{14,12},{16,18},{18,... | collective-permute-start | bytes 1382408 | tf_op jit(solution)/shard_map/ppermute | solution.py:88
  57.7 13.6 %copy-start.3 = (bf16[160,1440]{1,0:T(8,128)(2,1)}, bf16[160,1440]{1,0:T(8,128)(2,1)S(1)}, u32[]{:S(2)}) copy-start(bf16[160,1440]{1,0:T(8,128)(2,1)S(1)} %collective-permute-done.4.refs_1_) | copy-start | bytes 1382404
  57.7 14.8 %collective-permute-start.6 = (bf16[160,1440]{1,0:T(8,128)(2,1)S(1)}, bf16[160,1440]{1,0:T(8,128)(2,1)}, u32[]{:S(2)}, u32[]{:S(2)}) collective-permute-start(bf16[160,1440]{1,0:T(8,128)(2,1)S(1)} %collective-permute-done.4.refs_1_), channel_id=1, source_target_pairs={{0,2},{2,0},{4,6},{6,4},{8,10},{10,8},{12,14},{14,12},{16,18},{18,... | collective-permute-start | bytes 1382408 | tf_op jit(solution)/shard_map/ppermute | solution.py:88
  72.0 9.7 %collective-permute-start.17 = (bf16[160,1440]{1,0:T(8,128)(2,1)S(1)}, bf16[160,1440]{1,0:T(8,128)(2,1)S(1)}, u32[]{:S(2)}, u32[]{:S(2)}) collective-permute-start(bf16[160,1440]{1,0:T(8,128)(2,1)S(1)} %constant_dynamic-update-slice_fusion.refs_0_), channel_id=1, source_target_pairs={{0,2},{2,0},{4,6},{6,4},{8,10},{10,8},{12,14},{14,12},{16,18},{18,... | collective-permute-start | bytes 1382408 | tf_op jit(solution)/shard_map/ppermute | solution.py:88
  72.2 9.5 %collective-permute-start.18 = (bf16[160,1440]{1,0:T(8,128)(2,1)S(1)}, bf16[160,1440]{1,0:T(8,128)(2,1)S(1)}, u32[]{:S(2)}, u32[]{:S(2)}) collective-permute-start(bf16[160,1440]{1,0:T(8,128)(2,1)S(1)} %collective-permute-done.16.refs_1_), channel_id=1, source_target_pairs={{0,2},{2,0},{4,6},{6,4},{8,10},{10,8},{12,14},{14,12},{16,18},{18,... | collective-permute-start | bytes 1382408 | tf_op jit(solution)/shard_map/ppermute | solution.py:88
  81.1 13.6 %collective-permute-start.7 = (bf16[320,720]{1,0:T(8,128)(2,1)}, bf16[320,720]{1,0:T(8,128)(2,1)S(1)}, u32[]{:S(2)}, u32[]{:S(2)}) collective-permute-start(bf16[320,720]{1,0:T(8,128)(2,1)} %shard_map.145.refs_0_), channel_id=1, source_target_pairs={{0,1},{1,0},{2,3},{3,2},{4,5},{5,4},{6,7},{7,6},{8,9},{9,8},{10,11... | collective-permute-start | bytes 1382408 | tf_op jit(solution)/shard_map/ppermute | solution.py:88
  91.8 13.3 %collective-permute-start.19 = (bf16[320,720]{1,0:T(8,128)(2,1)}, bf16[320,720]{1,0:T(8,128)(2,1)S(1)}, u32[]{:S(2)}, u32[]{:S(2)}) collective-permute-start(bf16[320,720]{1,0:T(8,128)(2,1)} %shard_map.147.refs_0_), channel_id=1, source_target_pairs={{0,1},{1,0},{2,3},{3,2},{4,5},{5,4},{6,7},{7,6},{8,9},{9,8},{10,11... | collective-permute-start | bytes 1382408 | tf_op jit(solution)/shard_map/ppermute | solution.py:88
  100.6 10.5 %collective-permute-start.8 = (bf16[160,1440]{1,0:T(8,128)(2,1)}, bf16[160,1440]{1,0:T(8,128)(2,1)S(1)}, u32[]{:S(2)}, u32[]{:S(2)}) collective-permute-start(bf16[160,1440]{1,0:T(8,128)(2,1)} %get-tuple-element.10), channel_id=1, source_target_pairs={{0,2},{2,0},{4,6},{6,4},{8,10},{10,8},{12,14},{14,12},{16,18},{18,... | collective-permute-start | bytes 1382408 | tf_op jit(solution)/shard_map/ppermute | solution.py:88
  111.1 2.1 %collective-permute-start.20 = (bf16[160,1440]{1,0:T(8,128)(2,1)}, bf16[160,1440]{1,0:T(8,128)(2,1)S(1)}, u32[]{:S(2)}, u32[]{:S(2)}) collective-permute-start(bf16[160,1440]{1,0:T(8,128)(2,1)} %get-tuple-element.12), channel_id=1, source_target_pairs={{0,2},{2,0},{4,6},{6,4},{8,10},{10,8},{12,14},{14,12},{16,18},{18,... | collective-permute-start | bytes 1382408 | tf_op jit(solution)/shard_map/ppermute | solution.py:88
  111.3 11.3 %collective-permute-start.9 = (bf16[40,1440]{1,0:T(8,128)(2,1)S(1)}, bf16[40,1440]{1,0:T(8,128)(2,1)S(1)}, u32[]{:S(2)}, u32[]{:S(2)}) collective-permute-start(bf16[40,1440]{1,0:T(8,128)(2,1)S(1)} %get-tuple-element.33), channel_id=1, source_target_pairs={{0,4},{2,6},{4,0},{6,2},{8,12},{10,14},{12,8},{14,10},{16,20},{18,... | collective-permute-start | bytes 345608 | tf_op jit(solution)/shard_map/ppermute | solution.py:88
  114.3 16.8 %collective-permute-start.21 = (bf16[40,1440]{1,0:T(8,128)(2,1)S(1)}, bf16[40,1440]{1,0:T(8,128)(2,1)S(1)}, u32[]{:S(2)}, u32[]{:S(2)}) collective-permute-start(bf16[40,1440]{1,0:T(8,128)(2,1)S(1)} %get-tuple-element.30), channel_id=1, source_target_pairs={{0,16},{2,18},{4,20},{6,22},{8,24},{10,26},{12,28},{14,30},{16,0},... | collective-permute-start | bytes 345608 | tf_op jit(solution)/shard_map/ppermute | solution.py:88
  119.5 10.1 %collective-permute-start.10 = (bf16[40,1440]{1,0:T(8,128)(2,1)S(1)}, bf16[40,1440]{1,0:T(8,128)(2,1)S(1)}, u32[]{:S(2)}, u32[]{:S(2)}) collective-permute-start(bf16[40,1440]{1,0:T(8,128)(2,1)S(1)} %get-tuple-element.32), channel_id=1, source_target_pairs={{0,8},{2,10},{4,12},{6,14},{8,0},{10,2},{12,4},{14,6},{16,24},{18,... | collective-permute-start | bytes 345608 | tf_op jit(solution)/shard_map/ppermute | solution.py:88
  119.5 11.6 %collective-permute-start.11 = (bf16[40,1440]{1,0:T(8,128)(2,1)S(1)}, bf16[40,1440]{1,0:T(8,128)(2,1)S(1)}, u32[]{:S(2)}, u32[]{:S(2)}) collective-permute-start(bf16[40,1440]{1,0:T(8,128)(2,1)S(1)} %get-tuple-element.31), channel_id=1, source_target_pairs={{0,12},{2,14},{4,8},{6,10},{8,4},{10,6},{12,0},{14,2},{16,28},{18,... | collective-permute-start | bytes 345608 | tf_op jit(solution)/shard_map/ppermute | solution.py:88
  121.6 9.7 %collective-permute-start.22 = (bf16[40,1440]{1,0:T(8,128)(2,1)S(1)}, bf16[40,1440]{1,0:T(8,128)(2,1)S(1)}, u32[]{:S(2)}, u32[]{:S(2)}) collective-permute-start(bf16[40,1440]{1,0:T(8,128)(2,1)S(1)} %get-tuple-element.29), channel_id=1, source_target_pairs={{0,20},{2,22},{4,16},{6,18},{8,28},{10,30},{12,24},{14,26},{16,4},... | collective-permute-start | bytes 345608 | tf_op jit(solution)/shard_map/ppermute | solution.py:88
  122.5 13.2 %collective-permute-start.23 = (bf16[40,1440]{1,0:T(8,128)(2,1)S(1)}, bf16[40,1440]{1,0:T(8,128)(2,1)S(1)}, u32[]{:S(2)}, u32[]{:S(2)}) collective-permute-start(bf16[40,1440]{1,0:T(8,128)(2,1)S(1)} %get-tuple-element.28), channel_id=1, source_target_pairs={{0,24},{2,26},{4,28},{6,30},{8,16},{10,18},{12,20},{14,22},{16,8},... | collective-permute-start | bytes 345608 | tf_op jit(solution)/shard_map/ppermute | solution.py:88
  129.6 8.1 %collective-permute-start.24 = (bf16[40,1440]{1,0:T(8,128)(2,1)S(1)}, bf16[40,1440]{1,0:T(8,128)(2,1)S(1)}, u32[]{:S(2)}, u32[]{:S(2)}) collective-permute-start(bf16[40,1440]{1,0:T(8,128)(2,1)S(1)} %get-tuple-element.27), channel_id=1, source_target_pairs={{0,28},{2,30},{4,24},{6,26},{8,20},{10,22},{12,16},{14,18},{16,12}... | collective-permute-start | bytes 345608 | tf_op jit(solution)/shard_map/ppermute | solution.py:88
  (8 other events, 37.9 us)
